TPU v7x, 32 devices: a whole 2x2x4 slice. The times are simulated.
32 devices in a mesh: dp: 8 (over y, x, core), tensor: 4 (over z).
Axes of the slice: x: 2, y: 2, z: 4, core: 2. Of those that a mesh axis runs over, the one named last changes fastest.
Arguments:
- hidden: bfloat16 [4096, 8192], P(('dp', 'tensor')), may hold values from -6 to 6
- norm_gain: float32 [8192], replicated, may hold values from 0.5 to 1.5
- tile_values: bfloat16 [4, 80, 128, 128], P('tensor', 'dp'), may hold values from -0.15625 to 0.15625
- tile_ids: int32 [4, 80], P('tensor', 'dp'), may hold values from 0 to 1279, as said below
- tile_counts: int32 [4, 8], P('tensor', 'dp'), may hold values from 5 to 10, as said below
- proj_grad: bfloat16 [4096, 10240], P('dp', 'tensor'), may hold values from -6 to 6
Outputs:
- projections: bfloat16 [4096, 10240], P('dp', 'tensor')
- hidden_grad: bfloat16 [4096, 8192], P(('dp', 'tensor'))
- tile_grads: float32 [4, 80, 128, 128], P('tensor', 'dp')
- gain_grad: float32 [8192], replicated
Inputs may be any that keep to these rules, and one draw needn't show every extreme that they name: `tile_ids`: within each tensor index the 80 block numbers are distinct; a slot's number holds whether or not the slot is live. `tile_counts`: for every tensor index some owner has all 10 slots live.
All inputs are finite; a program needn't handle non-finite values.
Results may differ from a plain program's by a relative error of at most 0.013.
Values may be sent and summed in bfloat16 or wider, within the bound.
A program may use at most 192 MiB of HBM per device.

v0:
```python
import math
import jax
import jax.numpy as jnp
from jax import lax
from jax.sharding import PartitionSpec as P

EPSILON = 1e-05


def normalize(source, norm_gain):
    source_f = source.astype(jnp.float32)
    inverse = lax.rsqrt(jnp.mean(source_f * source_f, axis=-1, keepdims=True) + EPSILON)
    return (source_f, inverse, (source_f * inverse * norm_gain).astype(jnp.bfloat16))


def selector(block_names, total_count):
    return (block_names[:, None] == jnp.arange(total_count, dtype=jnp.int32)[None, :]).astype(
        jnp.bfloat16
    )


def pick_tiles(blocks, block_names, total_count):
    chooser = selector(block_names, total_count)
    return jnp.einsum("nri,sr->nsi", blocks, chooser, preferred_element_type=jnp.float32).astype(
        jnp.bfloat16
    )


def place_tiles(values, block_names, total_count):
    chooser = selector(block_names, total_count)
    upper_half = values.astype(jnp.bfloat16)
    lower_half = (values - upper_half.astype(jnp.float32)).astype(jnp.bfloat16)
    placed = jnp.einsum("nsi,sr->nri", upper_half, chooser, preferred_element_type=jnp.float32)
    return placed + jnp.einsum(
        "nsi,sr->nri", lower_half, chooser, preferred_element_type=jnp.float32
    )


def over_groups(handler, running, tile_block, tile_names, anchor, slot_count):
    group_total = tile_names.shape[0] // slot_count

    def loop_step(group_idx, state):
        offset = group_idx * slot_count
        block_vals = lax.dynamic_slice_in_dim(tile_block, offset, slot_count, 0)
        block_names = lax.dynamic_slice_in_dim(tile_names, offset, slot_count, 0)
        return handler(state, block_vals, block_names, anchor + offset)

    return lax.fori_loop(0, group_total, loop_step, running)


def body(hidden, norm_gain, tile_values, tile_ids, tile_counts, proj_grad):
    model_width = hidden.shape[1]
    tile_size = tile_values.shape[-1]
    slot_count = tile_values.shape[1]
    seq_rows = proj_grad.shape[0]
    col_tiles = proj_grad.shape[1] // tile_size
    row_tiles = model_width // tile_size
    live_mask = (jnp.arange(slot_count) < tile_counts[0, 0]).astype(jnp.bfloat16)
    masked = tile_values[0] * live_mask[:, None, None]
    own_names = tile_ids[0]
    hidden_f, inverse, normed = normalize(hidden, norm_gain)
    gathered = lax.all_gather(normed, "tensor", axis=0, tiled=True)
    x_blocks = gathered.reshape(seq_rows, row_tiles, tile_size)
    g_blocks = proj_grad.reshape(seq_rows, col_tiles, tile_size)

    def forward_group(running, block_vals, block_names, offset):
        picked = pick_tiles(x_blocks, block_names // col_tiles, row_tiles)
        parts = jnp.einsum("nsi,sij->nsj", picked, block_vals, preferred_element_type=jnp.float32)
        return running + place_tiles(parts, block_names % col_tiles, col_tiles)

    start_out = jnp.zeros((seq_rows, col_tiles, tile_size), jnp.float32)
    all_vals, all_names = (
        lax.all_gather(masked, "dp", axis=0, tiled=True),
        lax.all_gather(own_names, "dp", axis=0, tiled=True),
    )
    outputs = over_groups(forward_group, start_out, all_vals, all_names, 0, slot_count)
    projections = outputs.reshape(seq_rows, col_tiles * tile_size).astype(jnp.bfloat16)
    slot_total_all = all_names.shape[0]

    def row_grad_of(g_part):

        def backward_group(local_grad, block_vals, block_names, offset):
            picked_g = pick_tiles(g_part, block_names % col_tiles, col_tiles)
            backward = jnp.einsum(
                "nsj,sij->nsi", picked_g, block_vals, preferred_element_type=jnp.float32
            )
            return local_grad + place_tiles(backward, block_names // col_tiles, row_tiles)

        start_grad = jnp.zeros((g_part.shape[0], row_tiles, tile_size), jnp.float32)
        local_grad = over_groups(backward_group, start_grad, all_vals, all_names, 0, slot_count)
        return local_grad.reshape(g_part.shape[0], model_width).astype(jnp.bfloat16)

    def tile_grad_of(weight_grad, x_part, g_part):

        def tile_group(tile_acc, block_vals, block_names, offset):
            picked_x = pick_tiles(x_part, block_names // col_tiles, row_tiles)
            picked_g = pick_tiles(g_part, block_names % col_tiles, col_tiles)
            tile_part = jnp.einsum(
                "nsi,nsj->sij", picked_x, picked_g, preferred_element_type=jnp.float32
            )
            current = lax.dynamic_slice_in_dim(tile_acc, offset, tile_part.shape[0], 0)
            return lax.dynamic_update_slice_in_dim(tile_acc, current + tile_part, offset, 0)

        return over_groups(tile_group, weight_grad, all_vals, all_names, 0, slot_count)

    block_rows = math.gcd(seq_rows, 256)
    start_tiles = jnp.zeros((slot_total_all, tile_size, tile_size), jnp.float32)

    def row_block(block_idx, state):
        row_grad, weight_grad = state
        begin = block_idx * block_rows
        x_part = lax.dynamic_slice_in_dim(x_blocks, begin, block_rows, 0)
        g_part = lax.dynamic_slice_in_dim(g_blocks, begin, block_rows, 0)
        rounded = row_grad_of(g_part)
        row_grad = lax.dynamic_update_slice_in_dim(row_grad, rounded, begin, 0)
        weight_grad = tile_grad_of(weight_grad, x_part, g_part)
        return (row_grad, weight_grad)

    initial_back = (jnp.zeros((seq_rows, model_width), jnp.bfloat16), start_tiles)
    row_grad, weight_grad = lax.fori_loop(0, seq_rows // block_rows, row_block, initial_back)
    row_sum = lax.psum_scatter(row_grad, "tensor", scatter_dimension=0, tiled=True).astype(
        jnp.float32
    )
    tile_sum = lax.psum_scatter(
        weight_grad.astype(jnp.bfloat16), "dp", scatter_dimension=0, tiled=True
    ).astype(jnp.float32)
    tile_grads = (tile_sum * live_mask.astype(jnp.float32)[:, None, None])[None]
    unit = hidden_f * inverse
    gain_part = jnp.sum(row_sum * unit, axis=0)
    gain_grad = lax.psum(gain_part, ("dp", "tensor"))
    scaled = row_sum * norm_gain
    hidden_grad = (
        inverse * (scaled - unit * jnp.mean(scaled * unit, axis=-1, keepdims=True))
    ).astype(jnp.bfloat16)
    return (projections, hidden_grad, tile_grads, gain_grad)


def solution(mesh):
    in_specs = (
        P(("dp", "tensor"), None),
        P(),
        P("tensor", "dp", None, None),
        P("tensor", "dp"),
        P("tensor", "dp"),
        P("dp", "tensor"),
    )
    out_specs = (P("dp", "tensor"), P(("dp", "tensor"), None), P("tensor", "dp", None, None), P())
    return jax.shard_map(body, mesh=mesh, in_specs=in_specs, out_specs=out_specs, check_vma=False)
```

profile of v0, /device:TPU:0, one launch (start us, length us, event | category | flops | bytes accessed | tf_op | source)
XLA Modules:
  0.0 951.3 jit_solution(16404277503629230293)
XLA Ops:
  20.3 9.5 all-reduce
  29.8 135.6 %all-gather.6.cloned.1.call-done = bf16[512,8192]{1,0:T(8,128)(2,1)} async-done(((bf16[128,8192]{1,0:T(8,128)(2,1)}), bf16[512,8192]{1,0:T(8,128)(2,1)}) %all-gather.6.cloned.1.call-update) | async-done | bytes 8388624 | tf_op jit(solution)/shard_map/all_gather | solution.py:62
  165.4 9.4 copy.42
  174.7 21.4 %all-gather.4.cloned.1.call-done = bf16[80,128,128]{2,1,0:T(8,128)(2,1)} async-done(((bf16[10,128,128]{2,1,0:T(8,128)(2,1)}), bf16[80,128,128]{2,1,0:T(8,128)(2,1)}) %all-gather.4.cloned.1.call-update) | async-done | bytes 2621456 | tf_op jit(solution)/shard_map/all_gather | solution.py:73
  203.4 463.0 %while.101 = (s32[]{:T(128)}, bf16[512,8192]{1,0:T(8,128)(2,1)}, f32[80,128,128]{2,1,0:T(8,128)}, bf16[512,20,128]{0,2,1:T(8,128)(2,1)}, s32[80]{0:T(128)S(1)}, ...) while((s32[]{:T(128)}, bf16[512,8192]{1,0:T(8,128)(2,1)}, ...), condition=%wide.region_8.9_spmd, body=%wide.region_3.8_spmd.sunk | while | flops 330664448 | bytes 85787744 | solution.py:120
  205.9 162.2 %while.103 = (s32[]{:T(128)}, f32[256,64,128]{2,1,0:T(8,128)}, s32[80]{0:T(128)S(1)}, bf16[80,128,128]{2,1,0:T(8,128)(2,1)}, bf16[256,20,128]{2,1,0:T(8,128)(2,1...) while((s32[]{:T(128)}, f32[256,64,128]{2,1,0:T(8,128)}, s32[80]{0:T(128)S(1)}, ...), condition=%wide.region_5.5_spmd.clone, body=%wide.region_4.4_spmd.clone.sunk | while | flops 188810816 | bytes 41746828 | solution.py:48
  234.3 10.4 %bitcast_add_fusion.5 = f32[256,64,128]{2,1,0:T(8,128)} fusion(f32[256,64,128]{2,1,0:T(8,128)} %get-tuple-element.990, f32[64,256,128]{2,0,1:T(8,128)} %fusion.97, pred[]{:T(512)S(6)} %compare.7, bf16[256,10,128]{2,1,0:T(8,128)(2,1)S(1)} %copy.73, s32[10]{0:T(128)S(1)} %get-tuple-element.971), kind=kOutput, calls=%fused_computation.16.clone.1 | convolution fusion | flops 48235136 | bytes 25821224 | tf_op jit(solution)/shard_map/while/body/eval_jaxpr/while/body/eval_jaxpr/nsi,sr->nri/dot_general | solution.py:34
  254.8 10.4 %bitcast_add_fusion.5 = f32[256,64,128]{2,1,0:T(8,128)} fusion(f32[256,64,128]{2,1,0:T(8,128)} %get-tuple-element.990, f32[64,256,128]{2,0,1:T(8,128)} %fusion.97, pred[]{:T(512)S(6)} %compare.7, bf16[256,10,128]{2,1,0:T(8,128)(2,1)S(1)} %copy.73, s32[10]{0:T(128)S(1)} %get-tuple-element.971), kind=kOutput, calls=%fused_computation.16.clone.1 | convolution fusion | flops 48235136 | bytes 25821224 | tf_op jit(solution)/shard_map/while/body/eval_jaxpr/while/body/eval_jaxpr/nsi,sr->nri/dot_general | solution.py:34
  275.4 10.4 %bitcast_add_fusion.5 = f32[256,64,128]{2,1,0:T(8,128)} fusion(f32[256,64,128]{2,1,0:T(8,128)} %get-tuple-element.990, f32[64,256,128]{2,0,1:T(8,128)} %fusion.97, pred[]{:T(512)S(6)} %compare.7, bf16[256,10,128]{2,1,0:T(8,128)(2,1)S(1)} %copy.73, s32[10]{0:T(128)S(1)} %get-tuple-element.971), kind=kOutput, calls=%fused_computation.16.clone.1 | convolution fusion | flops 48235136 | bytes 25821224 | tf_op jit(solution)/shard_map/while/body/eval_jaxpr/while/body/eval_jaxpr/nsi,sr->nri/dot_general | solution.py:34
  296.0 10.4 %bitcast_add_fusion.5 = f32[256,64,128]{2,1,0:T(8,128)} fusion(f32[256,64,128]{2,1,0:T(8,128)} %get-tuple-element.990, f32[64,256,128]{2,0,1:T(8,128)} %fusion.97, pred[]{:T(512)S(6)} %compare.7, bf16[256,10,128]{2,1,0:T(8,128)(2,1)S(1)} %copy.73, s32[10]{0:T(128)S(1)} %get-tuple-element.971), kind=kOutput, calls=%fused_computation.16.clone.1 | convolution fusion | flops 48235136 | bytes 25821224 | tf_op jit(solution)/shard_map/while/body/eval_jaxpr/while/body/eval_jaxpr/nsi,sr->nri/dot_general | solution.py:34
  316.5 10.4 %bitcast_add_fusion.5 = f32[256,64,128]{2,1,0:T(8,128)} fusion(f32[256,64,128]{2,1,0:T(8,128)} %get-tuple-element.990, f32[64,256,128]{2,0,1:T(8,128)} %fusion.97, pred[]{:T(512)S(6)} %compare.7, bf16[256,10,128]{2,1,0:T(8,128)(2,1)S(1)} %copy.73, s32[10]{0:T(128)S(1)} %get-tuple-element.971), kind=kOutput, calls=%fused_computation.16.clone.1 | convolution fusion | flops 48235136 | bytes 25821224 | tf_op jit(solution)/shard_map/while/body/eval_jaxpr/while/body/eval_jaxpr/nsi,sr->nri/dot_general | solution.py:34
  337.1 10.4 %bitcast_add_fusion.5 = f32[256,64,128]{2,1,0:T(8,128)} fusion(f32[256,64,128]{2,1,0:T(8,128)} %get-tuple-element.990, f32[64,256,128]{2,0,1:T(8,128)} %fusion.97, pred[]{:T(512)S(6)} %compare.7, bf16[256,10,128]{2,1,0:T(8,128)(2,1)S(1)} %copy.73, s32[10]{0:T(128)S(1)} %get-tuple-element.971), kind=kOutput, calls=%fused_computation.16.clone.1 | convolution fusion | flops 48235136 | bytes 25821224 | tf_op jit(solution)/shard_map/while/body/eval_jaxpr/while/body/eval_jaxpr/nsi,sr->nri/dot_general | solution.py:34
  357.7 10.4 %bitcast_add_fusion.5 = f32[256,64,128]{2,1,0:T(8,128)} fusion(f32[256,64,128]{2,1,0:T(8,128)} %get-tuple-element.990, f32[64,256,128]{2,0,1:T(8,128)} %fusion.97, pred[]{:T(512)S(6)} %compare.7, bf16[256,10,128]{2,1,0:T(8,128)(2,1)S(1)} %copy.73, s32[10]{0:T(128)S(1)} %get-tuple-element.971), kind=kOutput, calls=%fused_computation.16.clone.1 | convolution fusion | flops 48235136 | bytes 25821224 | tf_op jit(solution)/shard_map/while/body/eval_jaxpr/while/body/eval_jaxpr/nsi,sr->nri/dot_general | solution.py:34
  372.5 10.0 %bitcast_dynamic-update-slice_fusion.3 = bf16[512,8192]{1,0:T(8,128)(2,1)} fusion(bf16[512,8192]{1,0:T(8,128)(2,1)} %get-tuple-element.1081, s32[]{:T(128)S(6)} %select_n.148, bf16[32,8,64,128]{3,2,1,0:T(8,128)(2,1)S(1)} %bitcast.116), kind=kLoop, calls=%fused_computation.34.clone.1 | loop fusion | bytes 8388612 | tf_op jit(solution)/shard_map/while/body/eval_jaxpr/dynamic_update_slice | solution.py:115
  387.7 47.1 %while.104 = (s32[]{:T(128)}, f32[80,128,128]{2,1,0:T(8,128)}, s32[80]{0:T(128)S(1)}, bf16[256,64,128]{2,1,0:T(8,128)(2,1)}, bf16[256,20,128]{2,1,0:T(8,128)(2,1...) while((s32[]{:T(128)}, f32[80,128,128]{2,1,0:T(8,128)}, s32[80]{0:T(128)S(1)}, ...), condition=%wide.region_7.7_spmd, body=%wide.region_6.6_spmd.sunk | while | flops 139756480 | bytes 9437531 | solution.py:48
  437.4 162.2 %while.103 = (s32[]{:T(128)}, f32[256,64,128]{2,1,0:T(8,128)}, s32[80]{0:T(128)S(1)}, bf16[80,128,128]{2,1,0:T(8,128)(2,1)}, bf16[256,20,128]{2,1,0:T(8,128)(2,1...) while((s32[]{:T(128)}, f32[256,64,128]{2,1,0:T(8,128)}, s32[80]{0:T(128)S(1)}, ...), condition=%wide.region_5.5_spmd.clone, body=%wide.region_4.4_spmd.clone.sunk | while | flops 188810816 | bytes 41746828 | solution.py:48
  465.7 10.4 %bitcast_add_fusion.5 = f32[256,64,128]{2,1,0:T(8,128)} fusion(f32[256,64,128]{2,1,0:T(8,128)} %get-tuple-element.990, f32[64,256,128]{2,0,1:T(8,128)} %fusion.97, pred[]{:T(512)S(6)} %compare.7, bf16[256,10,128]{2,1,0:T(8,128)(2,1)S(1)} %copy.73, s32[10]{0:T(128)S(1)} %get-tuple-element.971), kind=kOutput, calls=%fused_computation.16.clone.1 | convolution fusion | flops 48235136 | bytes 25821224 | tf_op jit(solution)/shard_map/while/body/eval_jaxpr/while/body/eval_jaxpr/nsi,sr->nri/dot_general | solution.py:34
  486.3 10.4 %bitcast_add_fusion.5 = f32[256,64,128]{2,1,0:T(8,128)} fusion(f32[256,64,128]{2,1,0:T(8,128)} %get-tuple-element.990, f32[64,256,128]{2,0,1:T(8,128)} %fusion.97, pred[]{:T(512)S(6)} %compare.7, bf16[256,10,128]{2,1,0:T(8,128)(2,1)S(1)} %copy.73, s32[10]{0:T(128)S(1)} %get-tuple-element.971), kind=kOutput, calls=%fused_computation.16.clone.1 | convolution fusion | flops 48235136 | bytes 25821224 | tf_op jit(solution)/shard_map/while/body/eval_jaxpr/while/body/eval_jaxpr/nsi,sr->nri/dot_general | solution.py:34
  506.9 10.4 %bitcast_add_fusion.5 = f32[256,64,128]{2,1,0:T(8,128)} fusion(f32[256,64,128]{2,1,0:T(8,128)} %get-tuple-element.990, f32[64,256,128]{2,0,1:T(8,128)} %fusion.97, pred[]{:T(512)S(6)} %compare.7, bf16[256,10,128]{2,1,0:T(8,128)(2,1)S(1)} %copy.73, s32[10]{0:T(128)S(1)} %get-tuple-element.971), kind=kOutput, calls=%fused_computation.16.clone.1 | convolution fusion | flops 48235136 | bytes 25821224 | tf_op jit(solution)/shard_map/while/body/eval_jaxpr/while/body/eval_jaxpr/nsi,sr->nri/dot_general | solution.py:34
  527.4 10.4 %bitcast_add_fusion.5 = f32[256,64,128]{2,1,0:T(8,128)} fusion(f32[256,64,128]{2,1,0:T(8,128)} %get-tuple-element.990, f32[64,256,128]{2,0,1:T(8,128)} %fusion.97, pred[]{:T(512)S(6)} %compare.7, bf16[256,10,128]{2,1,0:T(8,128)(2,1)S(1)} %copy.73, s32[10]{0:T(128)S(1)} %get-tuple-element.971), kind=kOutput, calls=%fused_computation.16.clone.1 | convolution fusion | flops 48235136 | bytes 25821224 | tf_op jit(solution)/shard_map/while/body/eval_jaxpr/while/body/eval_jaxpr/nsi,sr->nri/dot_general | solution.py:34
  548.0 10.4 %bitcast_add_fusion.5 = f32[256,64,128]{2,1,0:T(8,128)} fusion(f32[256,64,128]{2,1,0:T(8,128)} %get-tuple-element.990, f32[64,256,128]{2,0,1:T(8,128)} %fusion.97, pred[]{:T(512)S(6)} %compare.7, bf16[256,10,128]{2,1,0:T(8,128)(2,1)S(1)} %copy.73, s32[10]{0:T(128)S(1)} %get-tuple-element.971), kind=kOutput, calls=%fused_computation.16.clone.1 | convolution fusion | flops 48235136 | bytes 25821224 | tf_op jit(solution)/shard_map/while/body/eval_jaxpr/while/body/eval_jaxpr/nsi,sr->nri/dot_general | solution.py:34
  568.6 10.4 %bitcast_add_fusion.5 = f32[256,64,128]{2,1,0:T(8,128)} fusion(f32[256,64,128]{2,1,0:T(8,128)} %get-tuple-element.990, f32[64,256,128]{2,0,1:T(8,128)} %fusion.97, pred[]{:T(512)S(6)} %compare.7, bf16[256,10,128]{2,1,0:T(8,128)(2,1)S(1)} %copy.73, s32[10]{0:T(128)S(1)} %get-tuple-element.971), kind=kOutput, calls=%fused_computation.16.clone.1 | convolution fusion | flops 48235136 | bytes 25821224 | tf_op jit(solution)/shard_map/while/body/eval_jaxpr/while/body/eval_jaxpr/nsi,sr->nri/dot_general | solution.py:34
  589.1 10.4 %bitcast_add_fusion.5 = f32[256,64,128]{2,1,0:T(8,128)} fusion(f32[256,64,128]{2,1,0:T(8,128)} %get-tuple-element.990, f32[64,256,128]{2,0,1:T(8,128)} %fusion.97, pred[]{:T(512)S(6)} %compare.7, bf16[256,10,128]{2,1,0:T(8,128)(2,1)S(1)} %copy.73, s32[10]{0:T(128)S(1)} %get-tuple-element.971), kind=kOutput, calls=%fused_computation.16.clone.1 | convolution fusion | flops 48235136 | bytes 25821224 | tf_op jit(solution)/shard_map/while/body/eval_jaxpr/while/body/eval_jaxpr/nsi,sr->nri/dot_general | solution.py:34
  604.0 10.1 %bitcast_dynamic-update-slice_fusion.3 = bf16[512,8192]{1,0:T(8,128)(2,1)} fusion(bf16[512,8192]{1,0:T(8,128)(2,1)} %get-tuple-element.1081, s32[]{:T(128)S(6)} %select_n.148, bf16[32,8,64,128]{3,2,1,0:T(8,128)(2,1)S(1)} %bitcast.116), kind=kLoop, calls=%fused_computation.34.clone.1 | loop fusion | bytes 8388612 | tf_op jit(solution)/shard_map/while/body/eval_jaxpr/dynamic_update_slice | solution.py:115
  619.2 47.1 %while.104 = (s32[]{:T(128)}, f32[80,128,128]{2,1,0:T(8,128)}, s32[80]{0:T(128)S(1)}, bf16[256,64,128]{2,1,0:T(8,128)(2,1)}, bf16[256,20,128]{2,1,0:T(8,128)(2,1...) while((s32[]{:T(128)}, f32[80,128,128]{2,1,0:T(8,128)}, s32[80]{0:T(128)S(1)}, ...), condition=%wide.region_7.7_spmd, body=%wide.region_6.6_spmd.sunk | while | flops 139756480 | bytes 9437531 | solution.py:48
  671.5 213.0 %while.102 = (s32[]{:T(128)}, f32[512,20,128]{2,1,0:T(8,128)}, s32[80]{0:T(128)S(1)}, bf16[80,128,128]{2,1,0:T(8,128)(2,1)}, bf16[512,64,128]{2,1,0:T(8,128)(2,1...) while((s32[]{:T(128)}, f32[512,20,128]{2,1,0:T(8,128)}, s32[80]{0:T(128)S(1)}, ...), condition=%wide.region_2.3_spmd.clone, body=%wide.region_1.2_spmd.clone.sunk | while | flops 311297152 | bytes 42795404 | solution.py:48
  714.7 9.2 bitcast_add_fusion.4
  741.7 9.0 bitcast_add_fusion.4
  795.3 9.0 bitcast_add_fusion.4
  822.2 9.0 bitcast_add_fusion.4
  848.9 9.0 bitcast_add_fusion.4
  899.9 40.2 %psum.7 = f32[8192]{0:T(1024)} all-reduce(f32[8192]{0:T(1024)S(1)} %get-tuple-element.743), channel_id=1, replica_groups=mesh['dp'=8,'tensor'=4] {'dp','tensor'}, use_global_device_ids=true, to_apply=%region_13.14 | all-reduce | flops 8192 | bytes 65536 | tf_op jit(solution)/shard_map/psum | solution.py:130
  (265 shorter events, 508.4 us)
Async XLA Ops:
  7.2 6.4 copy-start
  7.2 158.2 %all-gather.6.cloned.1.call-start = ((), (), s32[]{:S(2)}) async-start(), calls=%async_computation.3 | async-start | bytes 10485760 | tf_op jit(solution)/shard_map/all_gather | solution.py:62
  9.3 9.5 %copy-start.2 = (f32[128]{0:T(128)}, f32[128]{0:T(128)S(1)}, u32[]{:S(2)}) copy-start(f32[128]{0:T(128)S(1)} %add_rsqrt_fusion) | copy-start | bytes 1540
  12.8 6.0 copy-start.5
  12.9 7.4 copy-start.4
  12.9 183.3 %all-gather.4.cloned.1.call-start = ((), (), s32[]{:S(2)}) async-start(), calls=%async_computation.2 | async-start | bytes 2949120 | tf_op jit(solution)/shard_map/all_gather | solution.py:73
  14.4 879.8 %reduce-scatter.5.cloned.1.call-start = ((), (), s32[]{:S(2)}) async-start(), calls=%async_computation.5 | async-start | bytes 2949120 | tf_op jit(solution)/shard_map/reduce_scatter | solution.py:124
  670.9 225.2 %reduce-scatter.3.cloned.1.call-start = ((), (), s32[]{:S(2)}) async-start(), calls=%async_computation.4 | async-start | bytes 10485760 | tf_op jit(solution)/shard_map/reduce_scatter | solution.py:121
  889.8 6.3 copy-start.1
  889.8 6.3 copy-start.3
Sparse Core Ops, SparseCore 0:
  13.0 152.3 all-gather.5
  167.8 28.3 all-gather.3
  671.1 43.6 reduce-scatter.4
  717.0 144.4 reduce-scatter.2
where the time goes:
time: 955 us; the launch traced here: 951 us
  matrix products  535 us (56%)
  local copies, waits for them, and re-layouts  159 us (17%)
  waiting for transfers between devices  158 us (17%)
  blocking collectives  49.7 us (5%)
  other arithmetic  33.7 us (4%)
  between operations  15.2 us (2%)
    dot_general x24, matrix products, place_tiles(): jnp.einsum('nsi,sr->nri', lower_half, chooser, preferred_element_type=jnp...  232 us
    all_gather x1, waiting for transfers between devices, body(): gathered = lax.all_gather(normed, 'tensor', axis=0, tiled=True)  136 us
    dot_general x24, matrix products, place_tiles(): jnp.einsum('nsi,sr->nri', upper_half, chooser, preferred_element_type=jnp...  115 us
    dot_general x56, matrix products, pick_tiles(): jnp.einsum('nri,sr->nsi', blocks, chooser, preferred_element_type=jnp.flo...  99.9 us
    convert_element_type x24, local copies, waits for them, and re-layouts, place_tiles(): upper_half = values.astype(jnp.bfloat16)  53.1 us
    psum x1, blocking collectives, body(): gain_grad = lax.psum(gain_part, ('dp', 'tensor'))  40.2 us
    convert_element_type x24, local copies, waits for them, and re-layouts, place_tiles(): lower_half = (values - upper_half.astype(jnp.float32)).astype(jnp.bfloat16)  39.5 us
    dot_general x16, matrix products, tile_group(): jnp.einsum('nsi,nsj->sij', picked_x, picked_g, preferred_element_type=jnp...  38.1 us
  transfers between devices with their start and end apart: 4, of which 2 were waited for; matrix products, arithmetic and copies ran while one was open for 25% of the time, Pallas kernels for 0%

commit v1 on v0

--- a/solution.py
+++ b/solution.py
@@ -127,7 +127,7 @@
     tile_grads = (tile_sum * live_mask.astype(jnp.float32)[:, None, None])[None]
     unit = hidden_f * inverse
     gain_part = jnp.sum(row_sum * unit, axis=0)
-    gain_grad = lax.psum(gain_part, ("dp", "tensor"))
+    gain_grad = jnp.sum(lax.all_gather(gain_part, ("dp", "tensor")), axis=0)
     scaled = row_sum * norm_gain
     hidden_grad = (
         inverse * (scaled - unit * jnp.mean(scaled * unit, axis=-1, keepdims=True))

time: 955 us -> 952 us (level)
  waiting for transfers between devices: 158 us -> 209 us
  blocking collectives: 49.7 us -> 9.46 us
  matrix products: 535 us -> 525 us
    all_gather x0 -> x1, waiting for transfers between devices: none -> 49.9 us  [body(): gain_grad = jnp.sum(lax.all_gather(gain_part, ('dp', 'tensor')), axis=0)]
    psum x1 -> x0, blocking collectives: 40.2 us -> none  [body(): gain_grad = lax.psum(gain_part, ('dp', 'tensor'))]
    dot_general x24, matrix products: 115 us -> 102 us  [place_tiles(): jnp.einsum('nsi,sr->nri', upper_half, chooser, preferred_element_type=jnp...]
  transfers between devices with their start and end apart: 4 -> 5, of which waited for: 2 -> 3; matrix products, arithmetic and copies ran while one was open for 25% -> 24% of each run, Pallas kernels for 0% -> 0%
where the time goes in v1:
time: 952 us; the launch traced here: 948 us
  matrix products  525 us (55%)
  waiting for transfers between devices  209 us (22%)
  local copies, waits for them, and re-layouts  155 us (16%)
  other arithmetic  33.8 us (4%)
  between operations  15.2 us (2%)
    dot_general x24, matrix products, place_tiles(): jnp.einsum('nsi,sr->nri', lower_half, chooser, preferred_element_type=jnp...  226 us
    all_gather x1, waiting for transfers between devices, body(): gathered = lax.all_gather(normed, 'tensor', axis=0, tiled=True)  137 us
    dot_general x24, matrix products, place_tiles(): jnp.einsum('nsi,sr->nri', upper_half, chooser, preferred_element_type=jnp...  102 us
    dot_general x56, matrix products, pick_tiles(): jnp.einsum('nri,sr->nsi', blocks, chooser, preferred_element_type=jnp.flo...  100 us
    convert_element_type x24, local copies, waits for them, and re-layouts, place_tiles(): upper_half = values.astype(jnp.bfloat16)  55.8 us
    all_gather x1, waiting for transfers between devices, body(): gain_grad = jnp.sum(lax.all_gather(gain_part, ('dp', 'tensor')), axis=0)  49.9 us
    dot_general x16, matrix products, tile_group(): jnp.einsum('nsi,nsj->sij', picked_x, picked_g, preferred_element_type=jnp...  38.2 us
    dot_general x16, matrix products, backward_group(): jnp.einsum('nsj,sij->nsi', picked_g, block_vals, preferred_element_type=j...  34.7 us
  transfers between devices with their start and end apart: 5, of which 3 were waited for; matrix products, arithmetic and copies ran while one was open for 24% of the time, Pallas kernels for 0%

profile of v1, /device:TPU:0, one launch (start us, length us, event | category | flops | bytes accessed | tf_op | source)
XLA Modules:
  0.0 948.2 jit_solution(10364356110724506348)
XLA Ops:
  19.1 9.5 all-reduce
  28.6 137.4 %all-gather.8.cloned.1.call-done = bf16[512,8192]{1,0:T(8,128)(2,1)} async-done(((bf16[128,8192]{1,0:T(8,128)(2,1)}), bf16[512,8192]{1,0:T(8,128)(2,1)}) %all-gather.8.cloned.1.call-update) | async-done | bytes 8388624 | tf_op jit(solution)/shard_map/all_gather | solution.py:62
  166.0 9.4 copy.55
  175.4 21.4 %all-gather.6.cloned.1.call-done = bf16[80,128,128]{2,1,0:T(8,128)(2,1)} async-done(((bf16[10,128,128]{2,1,0:T(8,128)(2,1)}), bf16[80,128,128]{2,1,0:T(8,128)(2,1)}) %all-gather.6.cloned.1.call-update) | async-done | bytes 2621456 | tf_op jit(solution)/shard_map/all_gather | solution.py:73
  204.0 462.5 %while.101 = (s32[]{:T(128)}, bf16[512,8192]{1,0:T(8,128)(2,1)}, f32[80,128,128]{2,1,0:T(8,128)}, bf16[512,20,128]{0,2,1:T(8,128)(2,1)}, s32[80]{0:T(128)S(1)}, ...) while((s32[]{:T(128)}, bf16[512,8192]{1,0:T(8,128)(2,1)}, ...), condition=%wide.region_8.9_spmd, body=%wide.region_3.8_spmd.sunk | while | flops 330664448 | bytes 85787744 | solution.py:120
  206.6 161.9 %while.103 = (s32[]{:T(128)}, f32[256,64,128]{2,1,0:T(8,128)}, s32[80]{0:T(128)S(1)}, bf16[80,128,128]{2,1,0:T(8,128)(2,1)}, bf16[256,20,128]{2,1,0:T(8,128)(2,1...) while((s32[]{:T(128)}, f32[256,64,128]{2,1,0:T(8,128)}, s32[80]{0:T(128)S(1)}, ...), condition=%wide.region_5.5_spmd.clone, body=%wide.region_4.4_spmd.clone.sunk | while | flops 188810816 | bytes 41746828 | solution.py:48
  234.9 10.4 %bitcast_add_fusion.5 = f32[256,64,128]{2,1,0:T(8,128)} fusion(f32[256,64,128]{2,1,0:T(8,128)} %get-tuple-element.1006, f32[64,256,128]{2,0,1:T(8,128)} %fusion.97, pred[]{:T(512)S(6)} %compare.7, bf16[256,10,128]{2,1,0:T(8,128)(2,1)S(1)} %copy.86, s32[10]{0:T(128)S(1)} %get-tuple-element.987), kind=kOutput, calls=%fused_computation.16.clone.1 | convolution fusion | flops 48235136 | bytes 25821224 | tf_op jit(solution)/shard_map/while/body/eval_jaxpr/while/body/eval_jaxpr/nsi,sr->nri/dot_general | solution.py:34
  255.4 10.4 %bitcast_add_fusion.5 = f32[256,64,128]{2,1,0:T(8,128)} fusion(f32[256,64,128]{2,1,0:T(8,128)} %get-tuple-element.1006, f32[64,256,128]{2,0,1:T(8,128)} %fusion.97, pred[]{:T(512)S(6)} %compare.7, bf16[256,10,128]{2,1,0:T(8,128)(2,1)S(1)} %copy.86, s32[10]{0:T(128)S(1)} %get-tuple-element.987), kind=kOutput, calls=%fused_computation.16.clone.1 | convolution fusion | flops 48235136 | bytes 25821224 | tf_op jit(solution)/shard_map/while/body/eval_jaxpr/while/body/eval_jaxpr/nsi,sr->nri/dot_general | solution.py:34
  276.0 10.4 %bitcast_add_fusion.5 = f32[256,64,128]{2,1,0:T(8,128)} fusion(f32[256,64,128]{2,1,0:T(8,128)} %get-tuple-element.1006, f32[64,256,128]{2,0,1:T(8,128)} %fusion.97, pred[]{:T(512)S(6)} %compare.7, bf16[256,10,128]{2,1,0:T(8,128)(2,1)S(1)} %copy.86, s32[10]{0:T(128)S(1)} %get-tuple-element.987), kind=kOutput, calls=%fused_computation.16.clone.1 | convolution fusion | flops 48235136 | bytes 25821224 | tf_op jit(solution)/shard_map/while/body/eval_jaxpr/while/body/eval_jaxpr/nsi,sr->nri/dot_general | solution.py:34
  296.5 10.4 %bitcast_add_fusion.5 = f32[256,64,128]{2,1,0:T(8,128)} fusion(f32[256,64,128]{2,1,0:T(8,128)} %get-tuple-element.1006, f32[64,256,128]{2,0,1:T(8,128)} %fusion.97, pred[]{:T(512)S(6)} %compare.7, bf16[256,10,128]{2,1,0:T(8,128)(2,1)S(1)} %copy.86, s32[10]{0:T(128)S(1)} %get-tuple-element.987), kind=kOutput, calls=%fused_computation.16.clone.1 | convolution fusion | flops 48235136 | bytes 25821224 | tf_op jit(solution)/shard_map/while/body/eval_jaxpr/while/body/eval_jaxpr/nsi,sr->nri/dot_general | solution.py:34
  317.0 10.4 %bitcast_add_fusion.5 = f32[256,64,128]{2,1,0:T(8,128)} fusion(f32[256,64,128]{2,1,0:T(8,128)} %get-tuple-element.1006, f32[64,256,128]{2,0,1:T(8,128)} %fusion.97, pred[]{:T(512)S(6)} %compare.7, bf16[256,10,128]{2,1,0:T(8,128)(2,1)S(1)} %copy.86, s32[10]{0:T(128)S(1)} %get-tuple-element.987), kind=kOutput, calls=%fused_computation.16.clone.1 | convolution fusion | flops 48235136 | bytes 25821224 | tf_op jit(solution)/shard_map/while/body/eval_jaxpr/while/body/eval_jaxpr/nsi,sr->nri/dot_general | solution.py:34
  337.5 10.4 %bitcast_add_fusion.5 = f32[256,64,128]{2,1,0:T(8,128)} fusion(f32[256,64,128]{2,1,0:T(8,128)} %get-tuple-element.1006, f32[64,256,128]{2,0,1:T(8,128)} %fusion.97, pred[]{:T(512)S(6)} %compare.7, bf16[256,10,128]{2,1,0:T(8,128)(2,1)S(1)} %copy.86, s32[10]{0:T(128)S(1)} %get-tuple-element.987), kind=kOutput, calls=%fused_computation.16.clone.1 | convolution fusion | flops 48235136 | bytes 25821224 | tf_op jit(solution)/shard_map/while/body/eval_jaxpr/while/body/eval_jaxpr/nsi,sr->nri/dot_general | solution.py:34
  358.1 10.4 %bitcast_add_fusion.5 = f32[256,64,128]{2,1,0:T(8,128)} fusion(f32[256,64,128]{2,1,0:T(8,128)} %get-tuple-element.1006, f32[64,256,128]{2,0,1:T(8,128)} %fusion.97, pred[]{:T(512)S(6)} %compare.7, bf16[256,10,128]{2,1,0:T(8,128)(2,1)S(1)} %copy.86, s32[10]{0:T(128)S(1)} %get-tuple-element.987), kind=kOutput, calls=%fused_computation.16.clone.1 | convolution fusion | flops 48235136 | bytes 25821224 | tf_op jit(solution)/shard_map/while/body/eval_jaxpr/while/body/eval_jaxpr/nsi,sr->nri/dot_general | solution.py:34
  372.9 10.0 %bitcast_dynamic-update-slice_fusion.3 = bf16[512,8192]{1,0:T(8,128)(2,1)} fusion(bf16[512,8192]{1,0:T(8,128)(2,1)} %get-tuple-element.1097, s32[]{:T(128)S(6)} %select_n.148, bf16[32,8,64,128]{3,2,1,0:T(8,128)(2,1)S(1)} %bitcast.116), kind=kLoop, calls=%fused_computation.34.clone.1 | loop fusion | bytes 8388612 | tf_op jit(solution)/shard_map/while/body/eval_jaxpr/dynamic_update_slice | solution.py:115
  388.1 47.2 %while.104 = (s32[]{:T(128)}, f32[80,128,128]{2,1,0:T(8,128)}, s32[80]{0:T(128)S(1)}, bf16[256,64,128]{2,1,0:T(8,128)(2,1)}, bf16[256,20,128]{2,1,0:T(8,128)(2,1...) while((s32[]{:T(128)}, f32[80,128,128]{2,1,0:T(8,128)}, s32[80]{0:T(128)S(1)}, ...), condition=%wide.region_7.7_spmd, body=%wide.region_6.6_spmd.sunk | while | flops 139756480 | bytes 9437531 | solution.py:48
  437.8 161.9 %while.103 = (s32[]{:T(128)}, f32[256,64,128]{2,1,0:T(8,128)}, s32[80]{0:T(128)S(1)}, bf16[80,128,128]{2,1,0:T(8,128)(2,1)}, bf16[256,20,128]{2,1,0:T(8,128)(2,1...) while((s32[]{:T(128)}, f32[256,64,128]{2,1,0:T(8,128)}, s32[80]{0:T(128)S(1)}, ...), condition=%wide.region_5.5_spmd.clone, body=%wide.region_4.4_spmd.clone.sunk | while | flops 188810816 | bytes 41746828 | solution.py:48
  466.2 10.4 %bitcast_add_fusion.5 = f32[256,64,128]{2,1,0:T(8,128)} fusion(f32[256,64,128]{2,1,0:T(8,128)} %get-tuple-element.1006, f32[64,256,128]{2,0,1:T(8,128)} %fusion.97, pred[]{:T(512)S(6)} %compare.7, bf16[256,10,128]{2,1,0:T(8,128)(2,1)S(1)} %copy.86, s32[10]{0:T(128)S(1)} %get-tuple-element.987), kind=kOutput, calls=%fused_computation.16.clone.1 | convolution fusion | flops 48235136 | bytes 25821224 | tf_op jit(solution)/shard_map/while/body/eval_jaxpr/while/body/eval_jaxpr/nsi,sr->nri/dot_general | solution.py:34
  486.7 10.4 %bitcast_add_fusion.5 = f32[256,64,128]{2,1,0:T(8,128)} fusion(f32[256,64,128]{2,1,0:T(8,128)} %get-tuple-element.1006, f32[64,256,128]{2,0,1:T(8,128)} %fusion.97, pred[]{:T(512)S(6)} %compare.7, bf16[256,10,128]{2,1,0:T(8,128)(2,1)S(1)} %copy.86, s32[10]{0:T(128)S(1)} %get-tuple-element.987), kind=kOutput, calls=%fused_computation.16.clone.1 | convolution fusion | flops 48235136 | bytes 25821224 | tf_op jit(solution)/shard_map/while/body/eval_jaxpr/while/body/eval_jaxpr/nsi,sr->nri/dot_general | solution.py:34
  507.2 10.4 %bitcast_add_fusion.5 = f32[256,64,128]{2,1,0:T(8,128)} fusion(f32[256,64,128]{2,1,0:T(8,128)} %get-tuple-element.1006, f32[64,256,128]{2,0,1:T(8,128)} %fusion.97, pred[]{:T(512)S(6)} %compare.7, bf16[256,10,128]{2,1,0:T(8,128)(2,1)S(1)} %copy.86, s32[10]{0:T(128)S(1)} %get-tuple-element.987), kind=kOutput, calls=%fused_computation.16.clone.1 | convolution fusion | flops 48235136 | bytes 25821224 | tf_op jit(solution)/shard_map/while/body/eval_jaxpr/while/body/eval_jaxpr/nsi,sr->nri/dot_general | solution.py:34
  527.7 10.4 %bitcast_add_fusion.5 = f32[256,64,128]{2,1,0:T(8,128)} fusion(f32[256,64,128]{2,1,0:T(8,128)} %get-tuple-element.1006, f32[64,256,128]{2,0,1:T(8,128)} %fusion.97, pred[]{:T(512)S(6)} %compare.7, bf16[256,10,128]{2,1,0:T(8,128)(2,1)S(1)} %copy.86, s32[10]{0:T(128)S(1)} %get-tuple-element.987), kind=kOutput, calls=%fused_computation.16.clone.1 | convolution fusion | flops 48235136 | bytes 25821224 | tf_op jit(solution)/shard_map/while/body/eval_jaxpr/while/body/eval_jaxpr/nsi,sr->nri/dot_general | solution.py:34
  548.3 10.4 %bitcast_add_fusion.5 = f32[256,64,128]{2,1,0:T(8,128)} fusion(f32[256,64,128]{2,1,0:T(8,128)} %get-tuple-element.1006, f32[64,256,128]{2,0,1:T(8,128)} %fusion.97, pred[]{:T(512)S(6)} %compare.7, bf16[256,10,128]{2,1,0:T(8,128)(2,1)S(1)} %copy.86, s32[10]{0:T(128)S(1)} %get-tuple-element.987), kind=kOutput, calls=%fused_computation.16.clone.1 | convolution fusion | flops 48235136 | bytes 25821224 | tf_op jit(solution)/shard_map/while/body/eval_jaxpr/while/body/eval_jaxpr/nsi,sr->nri/dot_general | solution.py:34
  568.8 10.4 %bitcast_add_fusion.5 = f32[256,64,128]{2,1,0:T(8,128)} fusion(f32[256,64,128]{2,1,0:T(8,128)} %get-tuple-element.1006, f32[64,256,128]{2,0,1:T(8,128)} %fusion.97, pred[]{:T(512)S(6)} %compare.7, bf16[256,10,128]{2,1,0:T(8,128)(2,1)S(1)} %copy.86, s32[10]{0:T(128)S(1)} %get-tuple-element.987), kind=kOutput, calls=%fused_computation.16.clone.1 | convolution fusion | flops 48235136 | bytes 25821224 | tf_op jit(solution)/shard_map/while/body/eval_jaxpr/while/body/eval_jaxpr/nsi,sr->nri/dot_general | solution.py:34
  589.3 10.4 %bitcast_add_fusion.5 = f32[256,64,128]{2,1,0:T(8,128)} fusion(f32[256,64,128]{2,1,0:T(8,128)} %get-tuple-element.1006, f32[64,256,128]{2,0,1:T(8,128)} %fusion.97, pred[]{:T(512)S(6)} %compare.7, bf16[256,10,128]{2,1,0:T(8,128)(2,1)S(1)} %copy.86, s32[10]{0:T(128)S(1)} %get-tuple-element.987), kind=kOutput, calls=%fused_computation.16.clone.1 | convolution fusion | flops 48235136 | bytes 25821224 | tf_op jit(solution)/shard_map/while/body/eval_jaxpr/while/body/eval_jaxpr/nsi,sr->nri/dot_general | solution.py:34
  604.2 10.1 %bitcast_dynamic-update-slice_fusion.3 = bf16[512,8192]{1,0:T(8,128)(2,1)} fusion(bf16[512,8192]{1,0:T(8,128)(2,1)} %get-tuple-element.1097, s32[]{:T(128)S(6)} %select_n.148, bf16[32,8,64,128]{3,2,1,0:T(8,128)(2,1)S(1)} %bitcast.116), kind=kLoop, calls=%fused_computation.34.clone.1 | loop fusion | bytes 8388612 | tf_op jit(solution)/shard_map/while/body/eval_jaxpr/dynamic_update_slice | solution.py:115
  619.4 47.2 %while.104 = (s32[]{:T(128)}, f32[80,128,128]{2,1,0:T(8,128)}, s32[80]{0:T(128)S(1)}, bf16[256,64,128]{2,1,0:T(8,128)(2,1)}, bf16[256,20,128]{2,1,0:T(8,128)(2,1...) while((s32[]{:T(128)}, f32[80,128,128]{2,1,0:T(8,128)}, s32[80]{0:T(128)S(1)}, ...), condition=%wide.region_7.7_spmd, body=%wide.region_6.6_spmd.sunk | while | flops 139756480 | bytes 9437531 | solution.py:48
  671.8 198.4 %while.102 = (s32[]{:T(128)}, f32[512,20,128]{2,1,0:T(8,128)}, s32[80]{0:T(128)S(1)}, bf16[80,128,128]{2,1,0:T(8,128)(2,1)}, bf16[512,64,128]{2,1,0:T(8,128)(2,1...) while((s32[]{:T(128)}, f32[512,20,128]{2,1,0:T(8,128)}, s32[80]{0:T(128)S(1)}, ...), condition=%wide.region_2.3_spmd.clone, body=%wide.region_1.2_spmd.clone.sunk | while | flops 311297152 | bytes 42795404 | solution.py:48
  711.6 8.4 bitcast_add_fusion.4
  736.9 8.4 bitcast_add_fusion.4
  761.9 8.4 bitcast_add_fusion.4
  786.9 8.6 bitcast_add_fusion.4
  837.0 8.3 bitcast_add_fusion.4
  889.7 49.9 %all-gather.10.cloned.1.call-done = f32[262144]{0:T(1024)} async-done(((f32[8192]{0:T(1024)}), f32[262144]{0:T(1024)}) %all-gather.10.cloned.1.call-update) | async-done | bytes 1048592 | tf_op jit(solution)/shard_map/all_gather | solution.py:130
  (273 shorter events, 497.2 us)
Async XLA Ops:
  7.2 7.1 copy-start.2
  7.2 8.0 copy-start.1
  7.2 158.8 %all-gather.8.cloned.1.call-start = ((), (), s32[]{:S(2)}) async-start(), calls=%async_computation.3 | async-start | bytes 10485760 | tf_op jit(solution)/shard_map/all_gather | solution.py:62
  9.5 0.5 copy-start.4
  13.5 4.3 copy-start.7
  13.5 5.5 copy-start.6
  13.5 183.3 %all-gather.6.cloned.1.call-start = ((), (), s32[]{:S(2)}) async-start(), calls=%async_computation.2 | async-start | bytes 2949120 | tf_op jit(solution)/shard_map/all_gather | solution.py:73
  15.1 864.9 %reduce-scatter.5.cloned.1.call-start = ((), (), s32[]{:S(2)}) async-start(), calls=%async_computation.5 | async-start | bytes 2949120 | tf_op jit(solution)/shard_map/reduce_scatter | solution.py:124
  671.2 210.8 %reduce-scatter.3.cloned.1.call-start = ((), (), s32[]{:S(2)}) async-start(), calls=%async_computation.4 | async-start | bytes 10485760 | tf_op jit(solution)/shard_map/reduce_scatter | solution.py:121
  671.7 267.8 %all-gather.10.cloned.1.call-start = ((), (), s32[]{:S(2)}) async-start(), calls=%async_computation.6 | async-start | bytes 1081344 | tf_op jit(solution)/shard_map/all_gather | solution.py:130
  875.5 6.5 copy-start
  875.5 6.5 copy-start.3
  875.5 6.5 copy-start.5
Sparse Core Ops, SparseCore 0:
  13.7 152.3 all-gather.7
  168.5 28.3 all-gather.5
  671.3 43.6 reduce-scatter.4
  717.2 144.4 reduce-scatter.2
  885.8 53.6 all-gather.9
